TPU v7x, 512 devices: a whole 4x4x16 slice. The times are simulated.
512 devices in a mesh: freq: 16 (over y, x), patch: 32 (over z, core).
Axes of the slice: x: 4, y: 4, z: 16, core: 2. Of those that a mesh axis runs over, the one named last changes fastest.
Arguments:
- responses: bfloat16 [2048, 2, 2048], P('patch', None, 'freq'), may hold values from -6 to 6
- adjoints: bfloat16 [2048, 2, 2048], P('patch', None, 'freq'), may hold values from -6 to 6
- patch_shapes: bfloat16 [3072, 4, 48, 128], P('patch'), may hold values from -0.25 to 0.25
- block_lists: int32 [3072, 4], P('patch'), may hold values from 0 to 15
- block_counts: int32 [3072], P('patch'), may hold values from 1 to 4
- patch_sizes: int32 [3072], P('patch'), may hold values from 12 to 48
- owner_map: int32 [3072], P('patch'), may hold values from 0 to 3071, each once
Outputs:
- loss_gradient: float32 [3072], P('patch')
Inputs may be any that keep to these rules, and one draw needn't show every extreme that they name: `owner_map`: each patch appears once.
All inputs are finite; a program needn't handle non-finite values.
Results may differ from a plain program's by a relative error of at most 0.0003.
Values may be sent and summed in bfloat16 or wider, within the bound.
A program may use at most 64 MiB of HBM per device.

v0:
```python
import math
import jax
import jax.numpy as jnp
from jax import lax
from jax.sharding import PartitionSpec as P


def strain_terms(total, masked, blocks, resp_piece, adjo_piece, width):
    count = resp_piece.shape[0]
    modes = resp_piece.shape[2]
    patches = masked.shape[0]
    samples = masked.shape[2]
    step = math.gcd(count, 32)
    turns = count // step

    def one(index, carry):
        resp = lax.dynamic_slice_in_dim(resp_piece, index * step, step, 0).reshape(
            step * 2, modes // width, width
        )
        adjo = lax.dynamic_slice_in_dim(adjo_piece, index * step, step, 0).reshape(
            step * 2, modes // width, width
        )
        forward = jnp.einsum(
            "pksb,cpkb->cps", masked, resp[:, blocks, :], preferred_element_type=jnp.float32
        )
        backward = jnp.einsum(
            "pksb,cpkb->cps", masked, adjo[:, blocks, :], preferred_element_type=jnp.float32
        )
        forward = forward.reshape(step, 2, patches, samples)
        backward = backward.reshape(step, 2, patches, samples)
        cross = forward[:, 0] * backward[:, 1] - forward[:, 1] * backward[:, 0]
        return carry + jnp.sum(cross, axis=(0, 2))

    return lax.fori_loop(0, turns, one, total)


def body(responses, adjoints, patch_shapes, block_lists, block_counts, patch_sizes, owner_map):
    patch_dev, slots, samples, width = patch_shapes.shape
    slot_live = jnp.arange(slots, dtype=jnp.int32)[None, :] < block_counts[:, None]
    row_live = jnp.arange(samples, dtype=jnp.int32)[None, :] < patch_sizes[:, None]
    live = (slot_live[:, :, None, None] & row_live[:, None, :, None]).astype(jnp.bfloat16)
    masked = patch_shapes * live
    freqs = responses.shape[0] * lax.axis_size("patch")
    empty = jnp.zeros((patch_dev,), jnp.float32)
    regrouped = (
        lax.all_to_all(responses, "freq", split_axis=0, concat_axis=2, tiled=True),
        lax.all_to_all(adjoints, "freq", split_axis=0, concat_axis=2, tiled=True),
    )
    terms = strain_terms(
        empty,
        masked,
        block_lists,
        lax.all_gather(regrouped[0], "patch", axis=0, tiled=True),
        lax.all_gather(regrouped[1], "patch", axis=0, tiled=True),
        width,
    )
    terms = terms * (samples * freqs) ** (-0.5)
    patches = patch_dev * lax.axis_size("patch")
    columns = jnp.arange(patches, dtype=jnp.int32)
    onehot = (owner_map[:, None] == columns[None, :]).astype(jnp.float32)
    dense = jnp.dot(terms, onehot, precision=lax.Precision.HIGHEST)
    mine = lax.psum_scatter(dense, "patch", scatter_dimension=0, tiled=True)
    return lax.psum(mine, "freq")


def solution(mesh):
    placed = (
        P("patch", None, "freq"),
        P("patch", None, "freq"),
        P("patch", None, None, None),
        P("patch", None),
        P("patch"),
        P("patch"),
        P("patch"),
    )
    return jax.shard_map(body, mesh=mesh, in_specs=placed, out_specs=P("patch"), check_vma=False)
```

profile of v0, /device:TPU:32, one launch (start us, length us, event | category | flops | bytes accessed | tf_op | source)
XLA Modules:
  0.0 486.1 jit_solution(6683167722934066681)
XLA Ops:
  6.5 14.6 %all_to_all.36 = bf16[64,2,128]{2,1,0:T(2,128)(2,1)S(1)} all-to-all(bf16[64,2,128]{2,1,0:T(2,128)(2,1)} %param.9), channel_id=1, replica_groups=mesh['freq'=16,'patch'=32] {'freq'}, dimensions={0} | all-to-all | bytes 65536 | tf_op jit(solution)/shard_map/all_to_all | solution.py:46
  21.2 0.6 all_to_all.29
  21.9 11.0 %all_to_all.37 = bf16[64,2,128]{2,1,0:T(2,128)(2,1)S(1)} all-to-all(bf16[64,2,128]{2,1,0:T(2,128)(2,1)} %param.10), channel_id=1, replica_groups=mesh['freq'=16,'patch'=32] {'freq'}, dimensions={0} | all-to-all | bytes 65536 | tf_op jit(solution)/shard_map/all_to_all | solution.py:47
  32.9 0.6 all_to_all.33
  33.6 0.8 copy.28
  34.4 1.3 dynamic-slice
  36.3 0.7 iota_compare_fusion.2
  37.1 0.7 iota_compare_fusion.3
  37.8 0.2 and_convert_fusion
  38.0 6.3 %broadcast_multiply_fusion = bf16[96,4,48,128]{3,2,1,0:T(8,128)(2,1)} fusion(bf16[96,4,48,128]{3,2,1,0:T(8,128)(2,1)} %param.11, bf16[96,4,48]{2,1,0:T(4,128)(2,1)S(1)} %and_convert_fusion), kind=kLoop, calls=%fused_computation.14 | loop fusion | flops 2359296 | bytes 9474048 | tf_op jit(solution)/shard_map/mul | solution.py:42
  44.3 48.6 %all-gather.3.cloned.1.call-done = bf16[128,2,2048]{2,1,0:T(2,128)(2,1)} async-done(((bf16[4,2,2048]{2,1,0:T(2,128)(2,1)}), bf16[128,2,2048]{2,1,0:T(2,128)(2,1)}) %all-gather.3.cloned.1.call-update) | async-done | bytes 1048592 | tf_op jit(solution)/shard_map/all_gather | solution.py:53
  92.8 70.0 %all-gather.5.cloned.1.call-done = bf16[128,2,2048]{2,1,0:T(2,128)(2,1)} async-done(((bf16[4,2,2048]{2,1,0:T(2,128)(2,1)}), bf16[128,2,2048]{2,1,0:T(2,128)(2,1)}) %all-gather.5.cloned.1.call-update) | async-done | bytes 1048592 | tf_op jit(solution)/shard_map/all_gather | solution.py:54
  162.8 185.3 %while.14 = (s32[]{:T(128)}, f32[96]{0:T(128)S(1)}, bf16[128,2,2048]{2,1,0:T(2,128)(2,1)}, s32[96,4]{1,0:T(8,128)S(1)}, bf16[96,4,48,128]{3,2,1,0:T(8,128)(2,1)}...) while((s32[]{:T(128)}, f32[96]{0:T(128)S(1)}, ...), condition=%wide.region_2.0_spmd.clone, body=%wide.region_0.0_spmd.clone.sunk | while | flops 604571840 | bytes 59785376 | solution.py:34
  162.8 1.4 constant_dynamic-slice_fusion.3
  164.2 0.2 reshape.144
  164.5 0.1 reshape.145
  164.6 13.3 %gather_fusion = bf16[384,64,128]{2,1,0:T(8,128)(2,1)} fusion(bf16[64,16,128]{2,0,1:T(8,128)(2,1)S(1)} %copy.39, s32[1024]{0:T(1024)S(1)} %pad_clamp_fusion.2), kind=kCustom, calls=%fused_computation.1.clone.clone.1 | custom fusion | bytes 12584448 | tf_op jit(solution)/shard_map/while/body/eval_jaxpr/gather | solution.py:27
  177.9 5.9 %convolution_bitcast_fusion.4 = f32[64,96,48]{0,2,1:T(8,128)S(1)} fusion(bf16[64,96,4,128]{3,0,2,1:T(8,128)(2,1)} %bitcast.66, bf16[96,4,48,128]{3,2,1,0:T(8,128)(2,1)} %get-tuple-element.233), kind=kOutput, calls=%fused_computation.2.clone.1 | convolution fusion | flops 301989888 | bytes 12189696 | tf_op jit(solution)/shard_map/while/body/eval_jaxpr/pksb,cpkb->cps/dot_general | solution.py:26
  183.9 1.9 copy.40
  185.7 0.2 reshape.146
  185.9 0.1 copy.41
  186.0 13.3 %gather_fusion.1 = bf16[384,64,128]{2,1,0:T(8,128)(2,1)} fusion(bf16[64,16,128]{2,0,1:T(8,128)(2,1)S(1)} %copy.41, s32[1024]{0:T(1024)S(1)} %pad_clamp_fusion.2), kind=kCustom, calls=%fused_computation.clone.clone.1 | custom fusion | bytes 12584448 | tf_op jit(solution)/shard_map/while/body/eval_jaxpr/gather | solution.py:24
  199.3 5.9 %convolution_bitcast_fusion.5 = f32[64,96,48]{0,2,1:T(8,128)S(1)} fusion(bf16[64,96,4,128]{3,0,2,1:T(8,128)(2,1)} %bitcast.65, bf16[96,4,48,128]{3,2,1,0:T(8,128)(2,1)} %get-tuple-element.233), kind=kOutput, calls=%fused_computation.3.clone.1 | convolution fusion | flops 301989888 | bytes 12189696 | tf_op jit(solution)/shard_map/while/body/eval_jaxpr/pksb,cpkb->cps/dot_general | solution.py:23
  205.2 1.9 copy.42
  207.1 2.1 fusion.23
  209.2 1.4 constant_dynamic-slice_fusion.3
  210.6 0.2 reshape.144
  210.7 0.1 copy.39
  210.8 0.1 reshape.145
  210.9 13.3 %gather_fusion = bf16[384,64,128]{2,1,0:T(8,128)(2,1)} fusion(bf16[64,16,128]{2,0,1:T(8,128)(2,1)S(1)} %copy.39, s32[1024]{0:T(1024)S(1)} %pad_clamp_fusion.2), kind=kCustom, calls=%fused_computation.1.clone.clone.1 | custom fusion | bytes 12584448 | tf_op jit(solution)/shard_map/while/body/eval_jaxpr/gather | solution.py:27
  224.3 5.9 %convolution_bitcast_fusion.4 = f32[64,96,48]{0,2,1:T(8,128)S(1)} fusion(bf16[64,96,4,128]{3,0,2,1:T(8,128)(2,1)} %bitcast.66, bf16[96,4,48,128]{3,2,1,0:T(8,128)(2,1)} %get-tuple-element.233), kind=kOutput, calls=%fused_computation.2.clone.1 | convolution fusion | flops 301989888 | bytes 12189696 | tf_op jit(solution)/shard_map/while/body/eval_jaxpr/pksb,cpkb->cps/dot_general | solution.py:26
  230.2 1.9 copy.40
  232.0 0.2 reshape.146
  232.2 0.1 copy.41
  232.3 13.3 %gather_fusion.1 = bf16[384,64,128]{2,1,0:T(8,128)(2,1)} fusion(bf16[64,16,128]{2,0,1:T(8,128)(2,1)S(1)} %copy.41, s32[1024]{0:T(1024)S(1)} %pad_clamp_fusion.2), kind=kCustom, calls=%fused_computation.clone.clone.1 | custom fusion | bytes 12584448 | tf_op jit(solution)/shard_map/while/body/eval_jaxpr/gather | solution.py:24
  245.6 5.9 %convolution_bitcast_fusion.5 = f32[64,96,48]{0,2,1:T(8,128)S(1)} fusion(bf16[64,96,4,128]{3,0,2,1:T(8,128)(2,1)} %bitcast.65, bf16[96,4,48,128]{3,2,1,0:T(8,128)(2,1)} %get-tuple-element.233), kind=kOutput, calls=%fused_computation.3.clone.1 | convolution fusion | flops 301989888 | bytes 12189696 | tf_op jit(solution)/shard_map/while/body/eval_jaxpr/pksb,cpkb->cps/dot_general | solution.py:23
  251.5 1.9 copy.42
  253.4 2.1 fusion.23
  255.5 1.4 constant_dynamic-slice_fusion.3
  256.9 0.2 reshape.144
  257.2 0.1 reshape.145
  257.3 13.3 %gather_fusion = bf16[384,64,128]{2,1,0:T(8,128)(2,1)} fusion(bf16[64,16,128]{2,0,1:T(8,128)(2,1)S(1)} %copy.39, s32[1024]{0:T(1024)S(1)} %pad_clamp_fusion.2), kind=kCustom, calls=%fused_computation.1.clone.clone.1 | custom fusion | bytes 12584448 | tf_op jit(solution)/shard_map/while/body/eval_jaxpr/gather | solution.py:27
  270.6 5.9 %convolution_bitcast_fusion.4 = f32[64,96,48]{0,2,1:T(8,128)S(1)} fusion(bf16[64,96,4,128]{3,0,2,1:T(8,128)(2,1)} %bitcast.66, bf16[96,4,48,128]{3,2,1,0:T(8,128)(2,1)} %get-tuple-element.233), kind=kOutput, calls=%fused_computation.2.clone.1 | convolution fusion | flops 301989888 | bytes 12189696 | tf_op jit(solution)/shard_map/while/body/eval_jaxpr/pksb,cpkb->cps/dot_general | solution.py:26
  276.5 1.9 copy.40
  278.4 0.2 reshape.146
  278.6 13.3 %gather_fusion.1 = bf16[384,64,128]{2,1,0:T(8,128)(2,1)} fusion(bf16[64,16,128]{2,0,1:T(8,128)(2,1)S(1)} %copy.41, s32[1024]{0:T(1024)S(1)} %pad_clamp_fusion.2), kind=kCustom, calls=%fused_computation.clone.clone.1 | custom fusion | bytes 12584448 | tf_op jit(solution)/shard_map/while/body/eval_jaxpr/gather | solution.py:24
  291.9 5.9 %convolution_bitcast_fusion.5 = f32[64,96,48]{0,2,1:T(8,128)S(1)} fusion(bf16[64,96,4,128]{3,0,2,1:T(8,128)(2,1)} %bitcast.65, bf16[96,4,48,128]{3,2,1,0:T(8,128)(2,1)} %get-tuple-element.233), kind=kOutput, calls=%fused_computation.3.clone.1 | convolution fusion | flops 301989888 | bytes 12189696 | tf_op jit(solution)/shard_map/while/body/eval_jaxpr/pksb,cpkb->cps/dot_general | solution.py:23
  297.9 1.9 copy.42
  299.7 2.1 fusion.23
  301.8 1.4 constant_dynamic-slice_fusion.3
  303.2 0.2 reshape.144
  303.5 0.1 reshape.145
  303.6 13.3 %gather_fusion = bf16[384,64,128]{2,1,0:T(8,128)(2,1)} fusion(bf16[64,16,128]{2,0,1:T(8,128)(2,1)S(1)} %copy.39, s32[1024]{0:T(1024)S(1)} %pad_clamp_fusion.2), kind=kCustom, calls=%fused_computation.1.clone.clone.1 | custom fusion | bytes 12584448 | tf_op jit(solution)/shard_map/while/body/eval_jaxpr/gather | solution.py:27
  316.9 5.9 %convolution_bitcast_fusion.4 = f32[64,96,48]{0,2,1:T(8,128)S(1)} fusion(bf16[64,96,4,128]{3,0,2,1:T(8,128)(2,1)} %bitcast.66, bf16[96,4,48,128]{3,2,1,0:T(8,128)(2,1)} %get-tuple-element.233), kind=kOutput, calls=%fused_computation.2.clone.1 | convolution fusion | flops 301989888 | bytes 12189696 | tf_op jit(solution)/shard_map/while/body/eval_jaxpr/pksb,cpkb->cps/dot_general | solution.py:26
  322.8 1.9 copy.40
  324.7 0.2 reshape.146
  325.0 13.3 %gather_fusion.1 = bf16[384,64,128]{2,1,0:T(8,128)(2,1)} fusion(bf16[64,16,128]{2,0,1:T(8,128)(2,1)S(1)} %copy.41, s32[1024]{0:T(1024)S(1)} %pad_clamp_fusion.2), kind=kCustom, calls=%fused_computation.clone.clone.1 | custom fusion | bytes 12584448 | tf_op jit(solution)/shard_map/while/body/eval_jaxpr/gather | solution.py:24
  338.3 5.9 %convolution_bitcast_fusion.5 = f32[64,96,48]{0,2,1:T(8,128)S(1)} fusion(bf16[64,96,4,128]{3,0,2,1:T(8,128)(2,1)} %bitcast.65, bf16[96,4,48,128]{3,2,1,0:T(8,128)(2,1)} %get-tuple-element.233), kind=kOutput, calls=%fused_computation.3.clone.1 | convolution fusion | flops 301989888 | bytes 12189696 | tf_op jit(solution)/shard_map/while/body/eval_jaxpr/pksb,cpkb->cps/dot_general | solution.py:23
  344.2 1.9 copy.42
  346.1 2.1 fusion.23
  348.2 0.5 fusion.3
  348.7 89.7 %all-reduce = f32[3072]{0:T(1024)S(1)} all-reduce(f32[3072]{0:T(1024)S(1)} %bitcast.73), channel_id=2, replica_groups=mesh['freq'=16,'patch'=32] {'patch'}, use_global_device_ids=true, to_apply=%region_3.0.clone | all-reduce | flops 3072 | bytes 24576
  438.4 0.1 dynamic-slice.1
  438.5 40.8 %psum.7 = f32[96]{0:T(128)} all-reduce(f32[96]{0:T(128)S(1)} %dynamic-slice.1), channel_id=1, replica_groups=mesh['freq'=16,'patch'=32] {'freq'}, use_global_device_ids=true, to_apply=%region_4.0 | all-reduce | flops 96 | bytes 768 | tf_op jit(solution)/shard_map/psum | solution.py:63
  (26 shorter events, 0.6 us)
Async XLA Ops:
  6.5 86.3 %all-gather.3.cloned.1.call-start = ((), (), s32[]{:S(2)}) async-start(), calls=%async_computation.2 | async-start | bytes 1081344 | tf_op jit(solution)/shard_map/all_gather | solution.py:53
  21.8 141.0 %all-gather.5.cloned.1.call-start = ((), (), s32[]{:S(2)}) async-start(), calls=%async_computation.3 | async-start | bytes 1081344 | tf_op jit(solution)/shard_map/all_gather | solution.py:54
  162.8 185.3 %copy-start = (s32[96]{0:T(128)S(1)}, s32[96]{0:T(128)}, u32[]{:S(2)}) copy-start(s32[96]{0:T(128)} %param.15) | copy-start | bytes 1156
Sparse Core Ops, SparseCore 0:
  22.0 70.8 all-gather.2
  95.0 67.8 all-gather.4
where the time goes:
time: 487 us; the launch traced here: 486 us
  blocking collectives  156 us (32%)
  local copies, waits for them, and re-layouts  133 us (27%)
  waiting for transfers between devices  119 us (24%)
  matrix products  47.9 us (10%)
  other arithmetic  16.3 us (3%)
  between operations  14.1 us (3%)
    unnamed x1, blocking collectives  89.7 us
    all_gather x1, waiting for transfers between devices, body(): lax.all_gather(regrouped[1], 'patch', axis=0, tiled=True)  70 us
    gather x4, local copies, waits for them, and re-layouts, one(): adjo[:, blocks, :]  53.2 us
    gather x4, local copies, waits for them, and re-layouts, one(): resp[:, blocks, :]  53.2 us
    all_gather x1, waiting for transfers between devices, body(): lax.all_gather(regrouped[0], 'patch', axis=0, tiled=True)  48.6 us
    psum x1, blocking collectives, body(): return lax.psum(mine, 'freq')  40.8 us
    dot_general x4, matrix products, one(): jnp.einsum('pksb,cpkb->cps', masked, adjo[:, blocks, :], preferred_elemen...  23.7 us
    dot_general x4, matrix products, one(): jnp.einsum('pksb,cpkb->cps', masked, resp[:, blocks, :], preferred_elemen...  23.7 us
  transfers between devices with their start and end apart: 2, of which 2 were waited for; matrix products, arithmetic and copies ran while one was open for 2% of the time, Pallas kernels for 0%

commit v1 on v0

--- a/solution.py
+++ b/solution.py
@@ -46,11 +46,28 @@
         lax.all_to_all(responses, "freq", split_axis=0, concat_axis=2, tiled=True),
         lax.all_to_all(adjoints, "freq", split_axis=0, concat_axis=2, tiled=True),
     )
+
+    def drive_unit(local_x, join_dim=0):
+        across = "patch"
+        far_arr, earlier = (lax.axis_size(across), lax.axis_index(across))
+        local_out, lower = (local_x, 1)
+        while lower < far_arr:
+            z2 = lax.ppermute(
+                local_out,
+                axis_name=across,
+                perm=list(map(lambda j0: (j0, j0 ^ lower), range(far_arr))),
+            )
+            s_next = jnp.concatenate([local_out, z2], axis=join_dim)
+            out_arr = jnp.concatenate([z2, local_out], join_dim)
+            local_out = jnp.where(earlier & lower == 0, s_next, out_arr)
+            lower = 2 * lower
+        return local_out
+
     terms = strain_terms(
         empty,
         masked,
         block_lists,
-        lax.all_gather(regrouped[0], "patch", axis=0, tiled=True),
+        drive_unit(regrouped[0]),
         lax.all_gather(regrouped[1], "patch", axis=0, tiled=True),
         width,
     )

time: 487 us -> 481 us (0.988)
  the two profiles are of different devices: /device:TPU:32 before, /device:TPU:2 now
where the time goes in v1:
time: 481 us
  blocking collectives  146 us (30%)
  local copies, waits for them, and re-layouts  132 us (27%)
  waiting for transfers between devices  70 us (15%)
  starting transfers between devices  49.3 us (10%)
  matrix products  47.9 us (10%)
  other arithmetic  21.6 us (4%)
  between operations  14.2 us (3%)
    unnamed x1, blocking collectives  91.5 us
    gather x4, local copies, waits for them, and re-layouts, one(): resp[:, blocks, :]  53.2 us
    gather x4, local copies, waits for them, and re-layouts, one(): adjo[:, blocks, :]  53.2 us
    ppermute x5, waiting for transfers between devices, drive_unit(): lax.ppermute(local_out, axis_name=across, perm=list(map(lambda j0: (j0, j...  50.8 us
    ppermute x5, starting transfers between devices, drive_unit(): lax.ppermute(local_out, axis_name=across, perm=list(map(lambda j0: (j0, j...  44.5 us
    psum x1, blocking collectives, body(): return lax.psum(mine, 'freq')  38.7 us
    dot_general x4, matrix products, one(): jnp.einsum('pksb,cpkb->cps', masked, adjo[:, blocks, :], preferred_elemen...  23.7 us
    dot_general x4, matrix products, one(): jnp.einsum('pksb,cpkb->cps', masked, resp[:, blocks, :], preferred_elemen...  23.7 us
  transfers between devices with their start and end apart: 7, of which 6 were waited for; matrix products, arithmetic and copies ran while one was open for 3% of the time, Pallas kernels for 0%

profile of v1, /device:TPU:2, one launch (start us, length us, event | category | flops | bytes accessed | tf_op | source)
XLA Modules:
  0.0 480.7 jit_solution(5774554216520176298)
XLA Ops:
  6.5 15.5 %all_to_all.36 = bf16[64,2,128]{2,1,0:T(2,128)(2,1)S(1)} all-to-all(bf16[64,2,128]{2,1,0:T(2,128)(2,1)} %param.9), channel_id=1, replica_groups=mesh['freq'=16,'patch'=32] {'freq'}, dimensions={0} | all-to-all | bytes 65536 | tf_op jit(solution)/shard_map/all_to_all | solution.py:46
  22.0 1.9 collective-permute-start
  24.0 1.2 collective-permute-done
  25.3 2.1 collective-permute-start.1
  27.4 4.8 all-to-all-start.1
  32.2 6.2 %all-to-all-done.1 = bf16[64,2,128]{2,1,0:T(2,128)(2,1)S(1)} async-done(((bf16[64,2,128]{2,1,0:T(2,128)(2,1)}), bf16[64,2,128]{2,1,0:T(2,128)(2,1)S(1)}, u32[]{:S(2)}, u32[]{:S(2)}) %all-to-all-start.1) | async-done | bytes 32800 | tf_op jit(solution)/shard_map/all_to_all | solution.py:47
  38.4 0.6 all_to_all.33
  39.1 0.3 broadcast_select_fusion.4
  39.4 5.2 %collective-permute-start.2 = (bf16[16,2,2048]{2,1,0:T(2,128)(2,1)S(1)}, bf16[16,2,2048]{2,1,0:T(2,128)(2,1)S(1)}, u32[]{:S(2)}, u32[]{:S(2)}) collective-permute-start(bf16[16,2,2048]{2,1,0:T(2,128)(2,1)S(1)} %broadcast_select_fusion.4), channel_id=1, source_target_pairs={{0,4},{1,5},{2,6},{3,7},{4,0},{5,1},{6,2},{7,3},{8,12},{9,13},{10,... | collective-permute-start | bytes 393224 | tf_op jit(solution)/shard_map/ppermute | solution.py:55
  44.6 0.7 iota_compare_fusion.2
  45.3 4.4 collective-permute-done.2
  49.8 0.6 broadcast_select_fusion.3
  50.4 8.9 %collective-permute-start.3 = (bf16[32,2,2048]{2,1,0:T(2,128)(2,1)S(1)}, bf16[32,2,2048]{2,1,0:T(2,128)(2,1)S(1)}, u32[]{:S(2)}, u32[]{:S(2)}) collective-permute-start(bf16[32,2,2048]{2,1,0:T(2,128)(2,1)S(1)} %broadcast_select_fusion.3), channel_id=1, source_target_pairs={{0,8},{1,9},{2,10},{3,11},{4,12},{5,13},{6,14},{7,15},{8,0},{9,1},... | collective-permute-start | bytes 786440 | tf_op jit(solution)/shard_map/ppermute | solution.py:55
  59.2 0.7 iota_compare_fusion.3
  60.0 0.8 copy.28
  60.8 1.3 dynamic-slice
  62.7 0.2 and_convert_fusion
  62.9 16.6 %collective-permute-done.3 = bf16[32,2,2048]{2,1,0:T(2,128)(2,1)S(1)} collective-permute-done((bf16[32,2,2048]{2,1,0:T(2,128)(2,1)S(1)}, bf16[32,2,2048]{2,1,0:T(2,128)(2,1)S(1)}, u32[]{:S(2)}, u32[]{:S(2)}) %collective-permute-start.3) | collective-permute-done | bytes 262176 | tf_op jit(solution)/shard_map/ppermute | solution.py:55
  79.5 1.2 broadcast_select_fusion.2
  80.7 26.4 %collective-permute-start.4 = (bf16[64,2,2048]{2,1,0:T(2,128)(2,1)S(1)}, bf16[64,2,2048]{2,1,0:T(2,128)(2,1)S(1)}, u32[]{:S(2)}, u32[]{:S(2)}) collective-permute-start(bf16[64,2,2048]{2,1,0:T(2,128)(2,1)S(1)} %broadcast_select_fusion.2), channel_id=1, source_target_pairs={{0,16},{1,17},{2,18},{3,19},{4,20},{5,21},{6,22},{7,23},{8,24},{9,... | collective-permute-start | bytes 1572872 | tf_op jit(solution)/shard_map/ppermute | solution.py:55
  107.1 6.2 %broadcast_multiply_fusion = bf16[96,4,48,128]{3,2,1,0:T(8,128)(2,1)} fusion(bf16[96,4,48,128]{3,2,1,0:T(8,128)(2,1)} %param.11, bf16[96,4,48]{2,1,0:T(4,128)(2,1)S(1)} %and_convert_fusion), kind=kLoop, calls=%fused_computation.14 | loop fusion | flops 2359296 | bytes 9474048 | tf_op jit(solution)/shard_map/mul | solution.py:42
  113.3 28.6 %collective-permute-done.4 = bf16[64,2,2048]{2,1,0:T(2,128)(2,1)S(1)} collective-permute-done((bf16[64,2,2048]{2,1,0:T(2,128)(2,1)S(1)}, bf16[64,2,2048]{2,1,0:T(2,128)(2,1)S(1)}, u32[]{:S(2)}, u32[]{:S(2)}) %collective-permute-start.4) | collective-permute-done | bytes 524320 | tf_op jit(solution)/shard_map/ppermute | solution.py:55
  141.9 3.1 broadcast_select_fusion.1
  145.1 12.9 %all-gather.2.cloned.1.call-done = bf16[128,2,2048]{2,1,0:T(2,128)(2,1)} async-done(((bf16[4,2,2048]{2,1,0:T(2,128)(2,1)}), bf16[128,2,2048]{2,1,0:T(2,128)(2,1)}) %all-gather.2.cloned.1.call-update) | async-done | bytes 1048592 | tf_op jit(solution)/shard_map/all_gather | solution.py:71
  158.0 185.0 %while.14 = (s32[]{:T(128)}, f32[96]{0:T(128)S(1)}, bf16[128,2,2048]{2,1,0:T(2,128)(2,1)}, s32[96,4]{1,0:T(8,128)S(1)}, bf16[96,4,48,128]{3,2,1,0:T(8,128)(2,1)}...) while((s32[]{:T(128)}, f32[96]{0:T(128)S(1)}, ...), condition=%wide.region_2.3_spmd.clone, body=%wide.region_0.2_spmd.clone.sunk | while | flops 604571840 | bytes 59785376 | solution.py:34
  158.0 1.4 constant_dynamic-slice_fusion.3
  159.4 0.2 reshape.144
  159.8 13.3 %gather_fusion = bf16[384,64,128]{2,1,0:T(8,128)(2,1)} fusion(bf16[64,16,128]{2,0,1:T(8,128)(2,1)S(1)} %copy.39, s32[1024]{0:T(1024)S(1)} %pad_clamp_fusion.2), kind=kCustom, calls=%fused_computation.1.clone.clone.1 | custom fusion | bytes 12584448 | tf_op jit(solution)/shard_map/while/body/eval_jaxpr/gather | solution.py:27
  173.1 5.9 %convolution_bitcast_fusion.4 = f32[64,96,48]{0,2,1:T(8,128)S(1)} fusion(bf16[64,96,4,128]{3,0,2,1:T(8,128)(2,1)} %bitcast.66, bf16[96,4,48,128]{3,2,1,0:T(8,128)(2,1)} %get-tuple-element.233), kind=kOutput, calls=%fused_computation.2.clone.1 | convolution fusion | flops 301989888 | bytes 12189696 | tf_op jit(solution)/shard_map/while/body/eval_jaxpr/pksb,cpkb->cps/dot_general | solution.py:26
  179.0 1.8 copy.40
  181.1 13.3 %gather_fusion.1 = bf16[384,64,128]{2,1,0:T(8,128)(2,1)} fusion(bf16[64,16,128]{2,0,1:T(8,128)(2,1)S(1)} %copy.41, s32[1024]{0:T(1024)S(1)} %pad_clamp_fusion.2), kind=kCustom, calls=%fused_computation.clone.clone.1 | custom fusion | bytes 12584448 | tf_op jit(solution)/shard_map/while/body/eval_jaxpr/gather | solution.py:24
  194.4 5.9 %convolution_bitcast_fusion.5 = f32[64,96,48]{0,2,1:T(8,128)S(1)} fusion(bf16[64,96,4,128]{3,0,2,1:T(8,128)(2,1)} %bitcast.65, bf16[96,4,48,128]{3,2,1,0:T(8,128)(2,1)} %get-tuple-element.233), kind=kOutput, calls=%fused_computation.3.clone.1 | convolution fusion | flops 301989888 | bytes 12189696 | tf_op jit(solution)/shard_map/while/body/eval_jaxpr/pksb,cpkb->cps/dot_general | solution.py:23
  200.3 1.8 copy.42
  202.2 2.1 fusion.23
  204.3 1.4 constant_dynamic-slice_fusion.3
  205.7 0.2 reshape.144
  206.1 13.3 %gather_fusion = bf16[384,64,128]{2,1,0:T(8,128)(2,1)} fusion(bf16[64,16,128]{2,0,1:T(8,128)(2,1)S(1)} %copy.39, s32[1024]{0:T(1024)S(1)} %pad_clamp_fusion.2), kind=kCustom, calls=%fused_computation.1.clone.clone.1 | custom fusion | bytes 12584448 | tf_op jit(solution)/shard_map/while/body/eval_jaxpr/gather | solution.py:27
  219.4 5.9 %convolution_bitcast_fusion.4 = f32[64,96,48]{0,2,1:T(8,128)S(1)} fusion(bf16[64,96,4,128]{3,0,2,1:T(8,128)(2,1)} %bitcast.66, bf16[96,4,48,128]{3,2,1,0:T(8,128)(2,1)} %get-tuple-element.233), kind=kOutput, calls=%fused_computation.2.clone.1 | convolution fusion | flops 301989888 | bytes 12189696 | tf_op jit(solution)/shard_map/while/body/eval_jaxpr/pksb,cpkb->cps/dot_general | solution.py:26
  225.3 1.8 copy.40
  227.4 13.3 %gather_fusion.1 = bf16[384,64,128]{2,1,0:T(8,128)(2,1)} fusion(bf16[64,16,128]{2,0,1:T(8,128)(2,1)S(1)} %copy.41, s32[1024]{0:T(1024)S(1)} %pad_clamp_fusion.2), kind=kCustom, calls=%fused_computation.clone.clone.1 | custom fusion | bytes 12584448 | tf_op jit(solution)/shard_map/while/body/eval_jaxpr/gather | solution.py:24
  240.7 5.9 %convolution_bitcast_fusion.5 = f32[64,96,48]{0,2,1:T(8,128)S(1)} fusion(bf16[64,96,4,128]{3,0,2,1:T(8,128)(2,1)} %bitcast.65, bf16[96,4,48,128]{3,2,1,0:T(8,128)(2,1)} %get-tuple-element.233), kind=kOutput, calls=%fused_computation.3.clone.1 | convolution fusion | flops 301989888 | bytes 12189696 | tf_op jit(solution)/shard_map/while/body/eval_jaxpr/pksb,cpkb->cps/dot_general | solution.py:23
  246.6 1.8 copy.42
  248.4 2.1 fusion.23
  250.5 1.4 constant_dynamic-slice_fusion.3
  251.9 0.2 reshape.144
  252.3 13.3 %gather_fusion = bf16[384,64,128]{2,1,0:T(8,128)(2,1)} fusion(bf16[64,16,128]{2,0,1:T(8,128)(2,1)S(1)} %copy.39, s32[1024]{0:T(1024)S(1)} %pad_clamp_fusion.2), kind=kCustom, calls=%fused_computation.1.clone.clone.1 | custom fusion | bytes 12584448 | tf_op jit(solution)/shard_map/while/body/eval_jaxpr/gather | solution.py:27
  265.6 5.9 %convolution_bitcast_fusion.4 = f32[64,96,48]{0,2,1:T(8,128)S(1)} fusion(bf16[64,96,4,128]{3,0,2,1:T(8,128)(2,1)} %bitcast.66, bf16[96,4,48,128]{3,2,1,0:T(8,128)(2,1)} %get-tuple-element.233), kind=kOutput, calls=%fused_computation.2.clone.1 | convolution fusion | flops 301989888 | bytes 12189696 | tf_op jit(solution)/shard_map/while/body/eval_jaxpr/pksb,cpkb->cps/dot_general | solution.py:26
  271.6 1.8 copy.40
  273.6 13.3 %gather_fusion.1 = bf16[384,64,128]{2,1,0:T(8,128)(2,1)} fusion(bf16[64,16,128]{2,0,1:T(8,128)(2,1)S(1)} %copy.41, s32[1024]{0:T(1024)S(1)} %pad_clamp_fusion.2), kind=kCustom, calls=%fused_computation.clone.clone.1 | custom fusion | bytes 12584448 | tf_op jit(solution)/shard_map/while/body/eval_jaxpr/gather | solution.py:24
  286.9 5.9 %convolution_bitcast_fusion.5 = f32[64,96,48]{0,2,1:T(8,128)S(1)} fusion(bf16[64,96,4,128]{3,0,2,1:T(8,128)(2,1)} %bitcast.65, bf16[96,4,48,128]{3,2,1,0:T(8,128)(2,1)} %get-tuple-element.233), kind=kOutput, calls=%fused_computation.3.clone.1 | convolution fusion | flops 301989888 | bytes 12189696 | tf_op jit(solution)/shard_map/while/body/eval_jaxpr/pksb,cpkb->cps/dot_general | solution.py:23
  292.9 1.8 copy.42
  294.7 2.1 fusion.23
  296.8 1.4 constant_dynamic-slice_fusion.3
  298.2 0.2 reshape.144
  298.6 13.3 %gather_fusion = bf16[384,64,128]{2,1,0:T(8,128)(2,1)} fusion(bf16[64,16,128]{2,0,1:T(8,128)(2,1)S(1)} %copy.39, s32[1024]{0:T(1024)S(1)} %pad_clamp_fusion.2), kind=kCustom, calls=%fused_computation.1.clone.clone.1 | custom fusion | bytes 12584448 | tf_op jit(solution)/shard_map/while/body/eval_jaxpr/gather | solution.py:27
  311.9 5.9 %convolution_bitcast_fusion.4 = f32[64,96,48]{0,2,1:T(8,128)S(1)} fusion(bf16[64,96,4,128]{3,0,2,1:T(8,128)(2,1)} %bitcast.66, bf16[96,4,48,128]{3,2,1,0:T(8,128)(2,1)} %get-tuple-element.233), kind=kOutput, calls=%fused_computation.2.clone.1 | convolution fusion | flops 301989888 | bytes 12189696 | tf_op jit(solution)/shard_map/while/body/eval_jaxpr/pksb,cpkb->cps/dot_general | solution.py:26
  317.8 1.8 copy.40
  319.9 13.3 %gather_fusion.1 = bf16[384,64,128]{2,1,0:T(8,128)(2,1)} fusion(bf16[64,16,128]{2,0,1:T(8,128)(2,1)S(1)} %copy.41, s32[1024]{0:T(1024)S(1)} %pad_clamp_fusion.2), kind=kCustom, calls=%fused_computation.clone.clone.1 | custom fusion | bytes 12584448 | tf_op jit(solution)/shard_map/while/body/eval_jaxpr/gather | solution.py:24
  333.2 5.9 %convolution_bitcast_fusion.5 = f32[64,96,48]{0,2,1:T(8,128)S(1)} fusion(bf16[64,96,4,128]{3,0,2,1:T(8,128)(2,1)} %bitcast.65, bf16[96,4,48,128]{3,2,1,0:T(8,128)(2,1)} %get-tuple-element.233), kind=kOutput, calls=%fused_computation.3.clone.1 | convolution fusion | flops 301989888 | bytes 12189696 | tf_op jit(solution)/shard_map/while/body/eval_jaxpr/pksb,cpkb->cps/dot_general | solution.py:23
  339.1 1.8 copy.42
  341.0 2.1 fusion.23
  343.1 0.5 fusion.3
  343.6 91.5 %all-reduce = f32[3072]{0:T(1024)S(1)} all-reduce(f32[3072]{0:T(1024)S(1)} %bitcast.73), channel_id=2, replica_groups=mesh['freq'=16,'patch'=32] {'patch'}, use_global_device_ids=true, to_apply=%region_3.4.clone | all-reduce | flops 3072 | bytes 24576
  435.2 38.7 %psum.7 = f32[96]{0:T(128)} all-reduce(f32[96]{0:T(128)S(1)} %dynamic-slice.1), channel_id=1, replica_groups=mesh['freq'=16,'patch'=32] {'freq'}, use_global_device_ids=true, to_apply=%region_4.5 | all-reduce | flops 96 | bytes 768 | tf_op jit(solution)/shard_map/psum | solution.py:80
  (39 shorter events, 2.1 us)
Async XLA Ops:
  22.0 3.1 collective-permute-start
  25.3 13.8 %collective-permute-start.1 = (bf16[8,2,2048]{2,1,0:T(2,128)(2,1)S(1)}, bf16[8,2,2048]{2,1,0:T(2,128)(2,1)S(1)}, u32[]{:S(2)}, u32[]{:S(2)}) collective-permute-start(bf16[8,2,2048]{2,1,0:T(2,128)(2,1)S(1)} %broadcast_select_fusion.5), channel_id=1, source_target_pairs={{0,2},{1,3},{2,0},{3,1},{4,6},{5,7},{6,4},{7,5},{8,10},{9,11},{10,... | collective-permute-start | bytes 196616 | tf_op jit(solution)/shard_map/ppermute | solution.py:55
  27.4 11.1 %all-to-all-start.1 = ((bf16[64,2,128]{2,1,0:T(2,128)(2,1)}), bf16[64,2,128]{2,1,0:T(2,128)(2,1)S(1)}, u32[]{:S(2)}, u32[]{:S(2)}) async-start(bf16[64,2,128]{2,1,0:T(2,128)(2,1)} %param.10), calls=%async_computation.1 | async-start | bytes 65536 | tf_op jit(solution)/shard_map/all_to_all | solution.py:47
  32.1 125.9 %all-gather.2.cloned.1.call-start = ((), (), s32[]{:S(2)}) async-start(), calls=%async_computation.2 | async-start | bytes 1081344 | tf_op jit(solution)/shard_map/all_gather | solution.py:71
  39.4 10.4 %collective-permute-start.2 = (bf16[16,2,2048]{2,1,0:T(2,128)(2,1)S(1)}, bf16[16,2,2048]{2,1,0:T(2,128)(2,1)S(1)}, u32[]{:S(2)}, u32[]{:S(2)}) collective-permute-start(bf16[16,2,2048]{2,1,0:T(2,128)(2,1)S(1)} %broadcast_select_fusion.4), channel_id=1, source_target_pairs={{0,4},{1,5},{2,6},{3,7},{4,0},{5,1},{6,2},{7,3},{8,12},{9,13},{10,... | collective-permute-start | bytes 393224 | tf_op jit(solution)/shard_map/ppermute | solution.py:55
  50.4 29.1 %collective-permute-start.3 = (bf16[32,2,2048]{2,1,0:T(2,128)(2,1)S(1)}, bf16[32,2,2048]{2,1,0:T(2,128)(2,1)S(1)}, u32[]{:S(2)}, u32[]{:S(2)}) collective-permute-start(bf16[32,2,2048]{2,1,0:T(2,128)(2,1)S(1)} %broadcast_select_fusion.3), channel_id=1, source_target_pairs={{0,8},{1,9},{2,10},{3,11},{4,12},{5,13},{6,14},{7,15},{8,0},{9,1},... | collective-permute-start | bytes 786440 | tf_op jit(solution)/shard_map/ppermute | solution.py:55
  80.7 61.3 %collective-permute-start.4 = (bf16[64,2,2048]{2,1,0:T(2,128)(2,1)S(1)}, bf16[64,2,2048]{2,1,0:T(2,128)(2,1)S(1)}, u32[]{:S(2)}, u32[]{:S(2)}) collective-permute-start(bf16[64,2,2048]{2,1,0:T(2,128)(2,1)S(1)} %broadcast_select_fusion.2), channel_id=1, source_target_pairs={{0,16},{1,17},{2,18},{3,19},{4,20},{5,21},{6,22},{7,23},{8,24},{9,... | collective-permute-start | bytes 1572872 | tf_op jit(solution)/shard_map/ppermute | solution.py:55
  158.0 185.1 %copy-start = (s32[96]{0:T(128)S(1)}, s32[96]{0:T(128)}, u32[]{:S(2)}) copy-start(s32[96]{0:T(128)} %param.15) | copy-start | bytes 1156
Sparse Core Ops, SparseCore 0:
  39.2 118.7 all-gather.1
